TPU v7x, 128 devices: a whole 4x4x4 slice. The times are simulated.
128 devices in a mesh: section: 4 (over y), expert: 32 (over x, z, core).
Axes of the slice: x: 4, y: 4, z: 4, core: 2. Of those that a mesh axis runs over, the one named last changes fastest.
Arguments:
- saved_inputs: bfloat16 [4, 2, 2048, 4096], P('section', None, 'expert'), may hold values from -6 to 6
- arriving: bfloat16 [4, 2048, 4096], P('section', 'expert'), may hold values from -1.5 to 1.5
- last_grad: bfloat16 [2048, 4096], P('expert'), may hold values from -1.5 to 1.5
- expert_ids: int32 [4, 2, 2048, 3], P('section', None, 'expert'), may hold values from 0 to 15, all different within a row; in each aligned block of 64 rows (0 to 63, 64 to 127, ..., all dimensions but the last counted through in order) at most 14 rows name the same one
- combine: bfloat16 [4, 2, 2048, 3], P('section', None, 'expert'), may hold values from 0.099609375 to 1
- w_gate: bfloat16 [4, 32, 4096, 384], P('section', 'expert'), may hold values from -0.09375 to 0.09375
- w_up: bfloat16 [4, 32, 4096, 384], P('section', 'expert'), may hold values from -0.09375 to 0.09375
- w_down: bfloat16 [4, 32, 384, 4096], P('section', 'expert'), may hold values from -0.21875 to 0.21875
Outputs:
- first_grads: bfloat16 [4, 2048, 4096], P('section', 'expert')
- second_grads: bfloat16 [4, 2048, 4096], P('section', 'expert')
- grad_gate: bfloat16 [4, 32, 4096, 384], P('section', 'expert')
- grad_up: bfloat16 [4, 32, 4096, 384], P('section', 'expert')
- grad_down: bfloat16 [4, 32, 384, 4096], P('section', 'expert')
Inputs may be any that keep to these rules, and one draw needn't show every extreme that they name: `expert_ids`: each token names 3 different experts. In every aligned block of 64 tokens (the tokens of one device in one section and micro-batch) no expert is named by more than 14 tokens, and in some blocks one expert is named by exactly 14.
All inputs are finite; a program needn't handle non-finite values.
Results may differ from a plain program's by a relative error of at most 0.0085.
Values may be sent and summed in bfloat16 or wider, within the bound.
A program may use at most 192 MiB of HBM per device.

v0:
```python
import jax
import jax.numpy as jnp
from jax import lax
from jax.sharding import PartitionSpec as P

HALVES = 2


def shifted(value, axis, by):
    count = lax.axis_size(axis)
    pairs = [(i, i + by) for i in range(count) if 0 <= i + by < count]
    return lax.ppermute(value, axis, pairs)


def rows_backward(x_rows, weighted, gate_w, up_w, down_w):
    gate_pre = jnp.dot(x_rows, gate_w, preferred_element_type=jnp.float32)
    up_pre = jnp.dot(x_rows, up_w, preferred_element_type=jnp.float32)
    gate_sigmoid = jax.nn.sigmoid(gate_pre)
    active = gate_pre * gate_sigmoid
    hidden = (active * up_pre).astype(jnp.bfloat16)
    contract = (((1,), (1,)), ((), ()))
    hidden_grad = lax.dot_general(weighted, down_w, contract, preferred_element_type=jnp.float32)
    gate_rows = (
        hidden_grad * up_pre * gate_sigmoid * (1.0 + gate_pre * (1.0 - gate_sigmoid))
    ).astype(jnp.bfloat16)
    up_rows = (hidden_grad * active).astype(jnp.bfloat16)
    partial_value = lax.dot_general(gate_rows, gate_w, contract, preferred_element_type=jnp.float32)
    partial_value = partial_value + lax.dot_general(
        up_rows, up_w, contract, preferred_element_type=jnp.float32
    )
    return (partial_value, hidden, gate_rows, up_rows)


def weight_terms(pieces):
    x_rows, weighted, hidden, gate_rows, up_rows = pieces
    across = (((0,), (0,)), ((), ()))
    return (
        lax.dot_general(x_rows, gate_rows, across, preferred_element_type=jnp.float32),
        lax.dot_general(x_rows, up_rows, across, preferred_element_type=jnp.float32),
        lax.dot_general(hidden, weighted, across, preferred_element_type=jnp.float32),
    )


def route_targets(route_ids, experts, capacity):
    tokens, top_count = route_ids.shape
    flat_ids = route_ids.reshape(tokens * top_count)
    onehot = (flat_ids[:, None] == jnp.arange(experts, dtype=jnp.int32)[None, :]).astype(jnp.int32)
    before = jnp.cumsum(onehot, axis=0) - onehot
    slot_index = jnp.sum(before * onehot, axis=1)
    return (flat_ids * capacity + slot_index).reshape(tokens, top_count)


def local(saved_inputs, arriving, last_grad, expert_ids, combine, w_gate, w_up, w_down):
    gate_w = w_gate[0, 0]
    up_w = w_up[0, 0]
    down_w = w_down[0, 0]
    tok_dev = arriving.shape[1]
    model_width = arriving.shape[2]
    top_count = expert_ids.shape[3]
    shards = lax.axis_size("expert")
    experts = shards // HALVES
    capacity = 5 * tok_dev * top_count // (4 * experts) // 2 * 2

    def section_pass(inputs, grads_in, route_ids, weights):
        target = route_targets(route_ids, experts, capacity)
        positions = jnp.arange(experts * capacity, dtype=jnp.int32)
        placed = target[None, :, :] == positions[:, None, None]
        picked = jnp.any(placed, axis=2).astype(jnp.bfloat16)
        scaled = jnp.sum(
            jnp.where(placed, weights[None, :, :].astype(jnp.float32), 0.0), axis=2
        ).astype(jnp.bfloat16)
        tables = jnp.stack([picked, scaled])
        sources = jnp.stack([inputs, grads_in])
        payload = jnp.einsum(
            "pqt,ptd->pqd", tables, sources, preferred_element_type=jnp.float32
        ).astype(jnp.bfloat16)
        spread = jnp.broadcast_to(
            payload.reshape(2, experts, 1, capacity, model_width),
            (2, experts, HALVES, capacity, model_width),
        )
        arrived = lax.all_to_all(
            spread.reshape(2, shards, capacity, model_width),
            "expert",
            split_axis=1,
            concat_axis=1,
            tiled=True,
        )
        x_rows = arrived[0].reshape(shards * capacity, model_width)
        weighted = arrived[1].reshape(shards * capacity, model_width)
        partial_value, hidden, gate_rows, up_rows = rows_backward(
            x_rows, weighted, gate_w, up_w, down_w
        )
        partial_value = partial_value.reshape(shards, capacity, model_width)
        returned_rows = lax.all_to_all(
            partial_value, "expert", split_axis=0, concat_axis=0, tiled=True
        )
        expert_rows = jnp.sum(
            returned_rows.reshape(experts, HALVES, capacity, model_width), axis=1
        ).astype(jnp.bfloat16)
        collect = jnp.any(target[:, :, None] == positions[None, None, :], axis=1).astype(
            jnp.bfloat16
        )
        expert_sum = jnp.dot(
            collect,
            expert_rows.reshape(experts * capacity, model_width),
            preferred_element_type=jnp.float32,
        )
        result = (grads_in.astype(jnp.float32) + expert_sum).astype(jnp.bfloat16)
        return (result, (x_rows, weighted, hidden, gate_rows, up_rows))

    section_last = lax.axis_index("section") == lax.axis_size("section") - 1
    first_grad, kept_first = section_pass(
        saved_inputs[0, 0], arriving[0], expert_ids[0, 0], combine[0, 0]
    )
    totals = weight_terms(kept_first)
    passed = shifted(first_grad, "section", -1)
    incoming = jnp.where(section_last, last_grad, passed)
    second_grad, kept_second = section_pass(
        saved_inputs[0, 1], incoming, expert_ids[0, 1], combine[0, 1]
    )
    second_terms = weight_terms(kept_second)
    totals = tuple((pair[0] + pair[1] for pair in zip(totals, second_terms)))
    return (
        first_grad[None],
        second_grad[None],
        totals[0].astype(jnp.bfloat16)[None, None],
        totals[1].astype(jnp.bfloat16)[None, None],
        totals[2].astype(jnp.bfloat16)[None, None],
    )


def solution(mesh):
    return jax.shard_map(
        local,
        mesh=mesh,
        in_specs=(
            P("section", None, "expert", None),
            P("section", "expert", None),
            P("expert", None),
            P("section", None, "expert", None),
            P("section", None, "expert", None),
            P("section", "expert", None, None),
            P("section", "expert", None, None),
            P("section", "expert", None, None),
        ),
        out_specs=(
            P("section", "expert", None),
            P("section", "expert", None),
            P("section", "expert", None, None),
            P("section", "expert", None, None),
            P("section", "expert", None, None),
        ),
        check_vma=False,
    )
```

profile of v0, /device:TPU:52, one launch (start us, length us, event | category | flops | bytes accessed | tf_op | source)
XLA Modules:
  0.0 666.0 jit_solution(7968685927313758433)
XLA Ops:
  13.5 7.1 %broadcast_in_dim.56 = bf16[2,16,2,14,4096]{4,0,3,2,1:T(2,128)(2,1)S(1)} broadcast(bf16[2,16,14,4096]{3,0,2,1:T(2,128)(2,1)S(1)} %bitcast.125), dimensions={0,1,3,4} | broadcast | bytes 11010048 | tf_op jit(solution)/shard_map/broadcast_in_dim | solution.py:77
  20.6 89.6 %all_to_all.20 = bf16[2,32,14,4096]{3,0,2,1:T(2,128)(2,1)S(1)} all-to-all(bf16[2,32,14,4096]{3,0,2,1:T(2,128)(2,1)S(1)} %bitcast.123), channel_id=1, replica_groups=mesh['section'=4,'expert'=32] {'expert'}, dimensions={1} | all-to-all | bytes 14680064 | tf_op jit(solution)/shard_map/all_to_all | solution.py:81
  110.2 36.9 %slice_reduce_fusion.3 = (bf16[32,14,4096]{2,1,0:T(8,128)(2,1)}, bf16[32,14,4096]{2,1,0:T(8,128)(2,1)}) fusion(bf16[2,32,14,4096]{3,0,2,1:T(2,128)(2,1)S(1)} %all_to_all.20), kind=kLoop, calls=%fused_computation.5 | loop fusion | bytes 14680064 | tf_op jit(solution)/shard_map/slice | solution.py:89
  152.1 5.1 fusion.10
  160.1 5.1 reshape_squeeze.14
  165.2 5.5 multiply_convert_fusion.4
  172.9 5.2 convolution_add_fusion.1
  178.1 6.9 %reshape.163 = f32[32,14,4096]{2,1,0:T(8,128)} reshape(f32[448,4096]{1,0:T(8,128)} %convolution_add_fusion.1) | data formatting | bytes 14680064 | tf_op jit(solution)/shard_map/reshape | solution.py:93
  184.9 8.0 %all-to-all-start.1 = ((f32[32,14,4096]{2,1,0:T(8,128)}), f32[32,14,4096]{2,1,0:T(8,128)}, u32[]{:S(2)}, u32[]{:S(2)}) async-start(f32[32,14,4096]{2,1,0:T(8,128)} %reshape.163), calls=%async_computation.1 | async-start | bytes 16777216 | tf_op jit(solution)/shard_map/all_to_all | solution.py:94
  193.1 124.2 %all-to-all-done.1 = f32[32,14,4096]{2,1,0:T(8,128)} async-done(((f32[32,14,4096]{2,1,0:T(8,128)}), f32[32,14,4096]{2,1,0:T(8,128)}, u32[]{:S(2)}, u32[]{:S(2)}) %all-to-all-start.1) | async-done | bytes 7340064 | tf_op jit(solution)/shard_map/all_to_all | solution.py:94
  317.3 6.0 bitcast_reduce_fusion.1
  331.6 12.8 %collective-permute-done = bf16[64,4096]{1,0:T(8,128)(2,1)} collective-permute-done((bf16[64,4096]{1,0:T(8,128)(2,1)}, bf16[64,4096]{1,0:T(8,128)(2,1)}, u32[]{:S(2)}, u32[]{:S(2)}) %collective-permute-start) | collective-permute-done | bytes 524320 | tf_op jit(solution)/shard_map/ppermute | solution.py:12
  351.6 7.1 %broadcast_in_dim.60 = bf16[2,16,2,14,4096]{4,0,3,2,1:T(2,128)(2,1)S(1)} broadcast(bf16[2,16,14,4096]{3,0,2,1:T(2,128)(2,1)S(1)} %bitcast.126), dimensions={0,1,3,4} | broadcast | bytes 11010048 | tf_op jit(solution)/shard_map/broadcast_in_dim | solution.py:77
  358.8 87.1 %all_to_all.21 = bf16[2,32,14,4096]{3,0,2,1:T(2,128)(2,1)S(1)} all-to-all(bf16[2,32,14,4096]{3,0,2,1:T(2,128)(2,1)S(1)} %bitcast.124), channel_id=1, replica_groups=mesh['section'=4,'expert'=32] {'expert'}, dimensions={1} | all-to-all | bytes 14680064 | tf_op jit(solution)/shard_map/all_to_all | solution.py:81
  445.9 36.9 %slice_reduce_fusion.1 = (bf16[32,14,4096]{2,1,0:T(8,128)(2,1)}, bf16[32,14,4096]{2,1,0:T(8,128)(2,1)}) fusion(bf16[2,32,14,4096]{3,0,2,1:T(2,128)(2,1)S(1)} %all_to_all.21), kind=kLoop, calls=%fused_computation.3 | loop fusion | bytes 14680064 | tf_op jit(solution)/shard_map/slice | solution.py:89
  482.8 5.0 reshape_squeeze.17
  487.8 6.1 fusion.13
  496.8 5.4 reshape_squeeze.16
  502.2 5.5 multiply_convert_fusion.2
  509.9 5.1 convolution_add_fusion
  515.0 6.8 %reshape.168 = f32[32,14,4096]{2,1,0:T(8,128)} reshape(f32[448,4096]{1,0:T(8,128)} %convolution_add_fusion) | data formatting | bytes 14680064 | tf_op jit(solution)/shard_map/reshape | solution.py:93
  521.8 8.2 %all-to-all-start.3 = ((f32[32,14,4096]{2,1,0:T(8,128)}), f32[32,14,4096]{2,1,0:T(8,128)}, u32[]{:S(2)}, u32[]{:S(2)}) async-start(f32[32,14,4096]{2,1,0:T(8,128)} %reshape.168), calls=%async_computation.3 | async-start | bytes 16777216 | tf_op jit(solution)/shard_map/all_to_all | solution.py:94
  551.8 102.3 %all-to-all-done.3 = f32[32,14,4096]{2,1,0:T(8,128)} async-done(((f32[32,14,4096]{2,1,0:T(8,128)}), f32[32,14,4096]{2,1,0:T(8,128)}, u32[]{:S(2)}, u32[]{:S(2)}) %all-to-all-start.3) | async-done | bytes 7340064 | tf_op jit(solution)/shard_map/all_to_all | solution.py:94
  654.1 6.1 bitcast_reduce_fusion
  (98 shorter events, 70.8 us)
Async XLA Ops:
  0.6 151.4 %copy-start = (bf16[1,1,4096,384]{3,2,1,0:T(8,128)(2,1)S(1)}, bf16[1,1,4096,384]{3,2,1,0:T(8,128)(2,1)}, u32[]{:S(2)}) copy-start(bf16[1,1,4096,384]{3,2,1,0:T(8,128)(2,1)} %param.13) | copy-start | bytes 9437188
  152.1 5.1 copy-start.3
  152.1 5.1 copy-start.7
  170.7 2.1 copy-start.12
  170.8 2.1 copy-start.8
  184.9 132.3 %all-to-all-start.1 = ((f32[32,14,4096]{2,1,0:T(8,128)}), f32[32,14,4096]{2,1,0:T(8,128)}, u32[]{:S(2)}, u32[]{:S(2)}) async-start(f32[32,14,4096]{2,1,0:T(8,128)} %reshape.163), calls=%async_computation.1 | async-start | bytes 16777216 | tf_op jit(solution)/shard_map/all_to_all | solution.py:94
  328.8 15.7 %collective-permute-start = (bf16[64,4096]{1,0:T(8,128)(2,1)}, bf16[64,4096]{1,0:T(8,128)(2,1)}, u32[]{:S(2)}, u32[]{:S(2)}) collective-permute-start(bf16[64,4096]{1,0:T(8,128)(2,1)} %fusion.3), channel_id=1, source_target_pairs={{32,0},{64,32},{96,64},{33,1},{65,33},{97,65},{34,2},{66,34},{98,6... | collective-permute-start | bytes 1572872 | tf_op jit(solution)/shard_map/ppermute | solution.py:12
  487.8 6.1 copy-start.1
  507.7 2.1 copy-start.14
  507.7 2.1 copy-start.10
  507.7 2.1 copy-start.9
  521.8 132.3 %all-to-all-start.3 = ((f32[32,14,4096]{2,1,0:T(8,128)}), f32[32,14,4096]{2,1,0:T(8,128)}, u32[]{:S(2)}, u32[]{:S(2)}) async-start(f32[32,14,4096]{2,1,0:T(8,128)} %reshape.168), calls=%async_computation.3 | async-start | bytes 16777216 | tf_op jit(solution)/shard_map/all_to_all | solution.py:94
  530.1 4.7 copy-start.4
  530.1 4.7 copy-start.13
  534.8 2.5 copy-start.5
  534.8 2.5 copy-start.16
  534.8 2.5 copy-start.17
  537.3 2.0 copy-start.2
  537.3 2.1 copy-start.11
  539.4 4.2 copy-start.15
  543.6 4.2 copy-start.6
  543.6 4.2 copy-start.18
  543.6 4.2 copy-start.19
where the time goes:
time: 672 us; the launch traced here: 666 us
  waiting for transfers between devices  239 us (36%)
  blocking collectives  177 us (26%)
  local copies, waits for them, and re-layouts  139 us (21%)
  matrix products  74 us (11%)
  starting transfers between devices  18.7 us (3%)
  other arithmetic  16.9 us (3%)
    all_to_all x2, waiting for transfers between devices, section_pass(): lax.all_to_all(partial_value, 'expert', split_axis=0, concat_axis=0, tile...  227 us
    all_to_all x2, blocking collectives, section_pass(): lax.all_to_all(spread.reshape(2, shards, capacity, model_width), 'expert'...  177 us
    slice x2, local copies, waits for them, and re-layouts, section_pass(): weighted = arrived[1].reshape(shards * capacity, model_width)  73.9 us
    all_to_all x2, starting transfers between devices, section_pass(): lax.all_to_all(partial_value, 'expert', split_axis=0, concat_axis=0, tile...  16.2 us
    broadcast_in_dim x2, local copies, waits for them, and re-layouts, section_pass(): jnp.broadcast_to(payload.reshape(2, experts, 1, capacity, model_width), (...  14.2 us
    reshape x2, local copies, waits for them, and re-layouts, section_pass(): partial_value = partial_value.reshape(shards, capacity, model_width)  13.7 us
  transfers between devices with their start and end apart: 3, of which 3 were waited for; matrix products, arithmetic and copies ran while one was open for 3% of the time, Pallas kernels for 0%

commit v1 on v0

--- a/solution.py
+++ b/solution.py
@@ -78,12 +78,20 @@
             payload.reshape(2, experts, 1, capacity, model_width),
             (2, experts, HALVES, capacity, model_width),
         )
-        arrived = lax.all_to_all(
-            spread.reshape(2, shards, capacity, model_width),
-            "expert",
-            split_axis=1,
-            concat_axis=1,
-            tiled=True,
+        arrived = jnp.concatenate(
+            lax.all_to_all(
+                jnp.stack(
+                    jnp.split(
+                        spread.reshape(2, shards, capacity, model_width),
+                        lax.axis_size("expert"),
+                        axis=1,
+                    )
+                ),
+                "expert",
+                0,
+                0,
+            ),
+            axis=1,
         )
         x_rows = arrived[0].reshape(shards * capacity, model_width)
         weighted = arrived[1].reshape(shards * capacity, model_width)

time: 672 us -> 688 us (1.024)
  local copies, waits for them, and re-layouts: 139 us -> 155 us
    unnamed x41 -> x103, local copies, waits for them, and re-layouts: 0.25 us -> 15.7 us
where the time goes in v1:
time: 688 us; the launch traced here: 682 us
  waiting for transfers between devices  239 us (35%)
  blocking collectives  177 us (26%)
  local copies, waits for them, and re-layouts  155 us (23%)
  matrix products  74 us (11%)
  starting transfers between devices  18.7 us (3%)
  other arithmetic  16.9 us (2%)
    all_to_all x2, waiting for transfers between devices, section_pass(): lax.all_to_all(partial_value, 'expert', split_axis=0, concat_axis=0, tile...  226 us
    all_to_all x2, blocking collectives, section_pass(): lax.all_to_all(jnp.stack(jnp.split(spread.reshape(2, shards, capacity, mo...  177 us
    slice x2, local copies, waits for them, and re-layouts, section_pass(): weighted = arrived[1].reshape(shards * capacity, model_width)  73.9 us
    all_to_all x2, starting transfers between devices, section_pass(): lax.all_to_all(partial_value, 'expert', split_axis=0, concat_axis=0, tile...  16.2 us
    unnamed x103, local copies, waits for them, and re-layouts  15.7 us
    broadcast_in_dim x2, local copies, waits for them, and re-layouts, section_pass(): jnp.broadcast_to(payload.reshape(2, experts, 1, capacity, model_width), (...  14.5 us
  transfers between devices with their start and end apart: 3, of which 3 were waited for; matrix products, arithmetic and copies ran while one was open for 3% of the time, Pallas kernels for 0%

profile of v1, /device:TPU:52, one launch (start us, length us, event | category | flops | bytes accessed | tf_op | source)
XLA Modules:
  0.0 682.5 jit_solution(15118912520696723312)
XLA Ops:
  13.5 7.4 %broadcast_in_dim.56 = bf16[2,16,2,14,4096]{4,0,3,2,1:T(2,128)(2,1)S(1)} broadcast(bf16[2,16,14,4096]{3,0,2,1:T(2,128)(2,1)S(1)} %bitcast.447), dimensions={0,1,3,4} | broadcast | bytes 11010048 | tf_op jit(solution)/shard_map/broadcast_in_dim | solution.py:77
  28.4 89.6 %all_to_all.20 = bf16[32,2,1,14,4096]{4,1,3,2,0:T(2,128)(2,1)S(1)} all-to-all(bf16[32,2,1,14,4096]{4,1,3,2,0:T(2,128)(2,1)S(1)} %fusion.64), channel_id=1, replica_groups=mesh['section'=4,'expert'=32] {'expert'}, dimensions={0} | all-to-all | bytes 14680064 | tf_op jit(solution)/shard_map/all_to_all | solution.py:82
  118.0 36.9 %slice_reduce_fusion.3 = (bf16[32,14,4096]{2,1,0:T(8,128)(2,1)}, bf16[32,14,4096]{2,1,0:T(8,128)(2,1)}) fusion(bf16[2,32,1,14,4096]{4,0,3,2,1:T(2,128)(2,1)S(1)} %bitcast.381), kind=kLoop, calls=%fused_computation.5 | loop fusion | bytes 14680064 | tf_op jit(solution)/shard_map/slice | solution.py:97
  154.9 5.0 reshape_squeeze.15
  159.9 5.1 fusion.10
  167.9 5.1 reshape_squeeze.14
  173.1 5.5 multiply_convert_fusion.4
  181.4 5.2 convolution_add_fusion.1
  186.6 6.9 %reshape.180 = f32[32,14,4096]{2,1,0:T(8,128)} reshape(f32[448,4096]{1,0:T(8,128)} %convolution_add_fusion.1) | data formatting | bytes 14680064 | tf_op jit(solution)/shard_map/reshape | solution.py:101
  193.5 8.0 %all-to-all-start.1 = ((f32[32,14,4096]{2,1,0:T(8,128)}), f32[32,14,4096]{2,1,0:T(8,128)}, u32[]{:S(2)}, u32[]{:S(2)}) async-start(f32[32,14,4096]{2,1,0:T(8,128)} %reshape.180), calls=%async_computation.1 | async-start | bytes 16777216 | tf_op jit(solution)/shard_map/all_to_all | solution.py:102
  201.6 124.2 %all-to-all-done.1 = f32[32,14,4096]{2,1,0:T(8,128)} async-done(((f32[32,14,4096]{2,1,0:T(8,128)}), f32[32,14,4096]{2,1,0:T(8,128)}, u32[]{:S(2)}, u32[]{:S(2)}) %all-to-all-start.1) | async-done | bytes 7340064 | tf_op jit(solution)/shard_map/all_to_all | solution.py:102
  325.8 6.0 bitcast_reduce_fusion.1
  340.2 12.8 %collective-permute-done = bf16[64,4096]{1,0:T(8,128)(2,1)} collective-permute-done((bf16[64,4096]{1,0:T(8,128)(2,1)}, bf16[64,4096]{1,0:T(8,128)(2,1)}, u32[]{:S(2)}, u32[]{:S(2)}) %collective-permute-start) | collective-permute-done | bytes 524320 | tf_op jit(solution)/shard_map/ppermute | solution.py:12
  360.2 7.1 %broadcast_in_dim.60 = bf16[2,16,2,14,4096]{4,0,3,2,1:T(2,128)(2,1)S(1)} broadcast(bf16[2,16,14,4096]{3,0,2,1:T(2,128)(2,1)S(1)} %bitcast.448), dimensions={0,1,3,4} | broadcast | bytes 11010048 | tf_op jit(solution)/shard_map/broadcast_in_dim | solution.py:77
  374.8 87.3 %all_to_all.21 = bf16[32,2,1,14,4096]{4,1,3,2,0:T(2,128)(2,1)S(1)} all-to-all(bf16[32,2,1,14,4096]{4,1,3,2,0:T(2,128)(2,1)S(1)} %fusion.32), channel_id=1, replica_groups=mesh['section'=4,'expert'=32] {'expert'}, dimensions={0} | all-to-all | bytes 14680064 | tf_op jit(solution)/shard_map/all_to_all | solution.py:82
  462.1 36.9 %slice_reduce_fusion.1 = (bf16[32,14,4096]{2,1,0:T(8,128)(2,1)}, bf16[32,14,4096]{2,1,0:T(8,128)(2,1)}) fusion(bf16[2,32,1,14,4096]{4,0,3,2,1:T(2,128)(2,1)S(1)} %bitcast.382), kind=kLoop, calls=%fused_computation.3 | loop fusion | bytes 14680064 | tf_op jit(solution)/shard_map/slice | solution.py:97
  499.0 5.0 reshape_squeeze.17
  504.0 6.1 fusion.13
  518.0 5.5 multiply_convert_fusion.2
  526.3 5.1 convolution_add_fusion
  531.4 6.8 %reshape.186 = f32[32,14,4096]{2,1,0:T(8,128)} reshape(f32[448,4096]{1,0:T(8,128)} %convolution_add_fusion) | data formatting | bytes 14680064 | tf_op jit(solution)/shard_map/reshape | solution.py:101
  538.3 8.2 %all-to-all-start.3 = ((f32[32,14,4096]{2,1,0:T(8,128)}), f32[32,14,4096]{2,1,0:T(8,128)}, u32[]{:S(2)}, u32[]{:S(2)}) async-start(f32[32,14,4096]{2,1,0:T(8,128)} %reshape.186), calls=%async_computation.3 | async-start | bytes 16777216 | tf_op jit(solution)/shard_map/all_to_all | solution.py:102
  568.3 102.3 %all-to-all-done.3 = f32[32,14,4096]{2,1,0:T(8,128)} async-done(((f32[32,14,4096]{2,1,0:T(8,128)}), f32[32,14,4096]{2,1,0:T(8,128)}, u32[]{:S(2)}, u32[]{:S(2)}) %all-to-all-start.3) | async-done | bytes 7340064 | tf_op jit(solution)/shard_map/all_to_all | solution.py:102
  670.6 6.1 bitcast_reduce_fusion
  (162 shorter events, 86.7 us)
Async XLA Ops:
  0.6 159.2 %copy-start = (bf16[1,1,4096,384]{3,2,1,0:T(8,128)(2,1)S(1)}, bf16[1,1,4096,384]{3,2,1,0:T(8,128)(2,1)}, u32[]{:S(2)}) copy-start(bf16[1,1,4096,384]{3,2,1,0:T(8,128)(2,1)} %param.13) | copy-start | bytes 9437188
  159.9 5.1 copy-start.3
  159.9 5.1 copy-start.7
  178.6 0.8 copy-start.12
  178.6 2.9 copy-start.8
  193.5 132.3 %all-to-all-start.1 = ((f32[32,14,4096]{2,1,0:T(8,128)}), f32[32,14,4096]{2,1,0:T(8,128)}, u32[]{:S(2)}, u32[]{:S(2)}) async-start(f32[32,14,4096]{2,1,0:T(8,128)} %reshape.180), calls=%async_computation.1 | async-start | bytes 16777216 | tf_op jit(solution)/shard_map/all_to_all | solution.py:102
  337.3 15.7 %collective-permute-start = (bf16[64,4096]{1,0:T(8,128)(2,1)}, bf16[64,4096]{1,0:T(8,128)(2,1)}, u32[]{:S(2)}, u32[]{:S(2)}) collective-permute-start(bf16[64,4096]{1,0:T(8,128)(2,1)} %fusion.3), channel_id=1, source_target_pairs={{32,0},{64,32},{96,64},{33,1},{65,33},{97,65},{34,2},{66,34},{98,6... | collective-permute-start | bytes 1572872 | tf_op jit(solution)/shard_map/ppermute | solution.py:12
  504.0 6.1 copy-start.1
  523.5 0.7 copy-start.14
  523.5 2.8 copy-start.10
  523.5 2.8 copy-start.9
  538.3 132.3 %all-to-all-start.3 = ((f32[32,14,4096]{2,1,0:T(8,128)}), f32[32,14,4096]{2,1,0:T(8,128)}, u32[]{:S(2)}, u32[]{:S(2)}) async-start(f32[32,14,4096]{2,1,0:T(8,128)} %reshape.186), calls=%async_computation.3 | async-start | bytes 16777216 | tf_op jit(solution)/shard_map/all_to_all | solution.py:102
  546.4 4.8 copy-start.4
  546.4 4.8 copy-start.13
  551.2 2.5 copy-start.5
  551.2 2.5 copy-start.16
  551.2 2.5 copy-start.17
  553.7 2.0 copy-start.2
  553.8 2.1 copy-start.11
  555.8 4.2 copy-start.15
  560.1 4.2 copy-start.6
  560.1 4.2 copy-start.18
  560.1 4.2 copy-start.19
